TPU v7x, 512 devices: a whole 4x4x16 slice. The times are simulated.
512 devices in a mesh: win: 16 (over z_lo, core), lat: 32 (over x, z_hi, y).
Axes of the slice: x: 4, y: 4, z: 16 (z_hi: 2, z_lo: 8; z = z_hi * 8 + z_lo), core: 2. Of those that a mesh axis runs over, the one named last changes fastest.
Arguments:
- perturbation: float32 [16, 256, 20, 768], P('win', 'lat'), may hold values from -6 to 6
- lat_offset: int32 [16, 256, 20, 768], P('win', 'lat'), may hold values from -1 to 0
- lon_offset: int32 [16, 256, 20, 768], P('win', 'lat'), may hold values from -4 to 3
- lat_weight: float32 [16, 256, 20, 768], P('win', 'lat'), may hold values from 0 to 0.3
- lon_weight: float32 [16, 256, 20, 768], P('win', 'lat'), may hold values from 0 to 0.3
- spectral_var: float32 [256, 768], P(None, 'lat'), may hold values from 0.5 to 4
Outputs:
- weighted_error: float32 [16, 256, 20, 768], P('win', 'lat')
All inputs are finite; a program needn't handle non-finite values.
Results may differ from a plain program's by a relative error of at most 0.0003.
Values sent between devices are 32-bit elements; how exact they have to be, the bound alone decides.
A program may use at most 64 MiB of HBM per device.

v0:
```python
import math

import jax
import jax.numpy as jnp
import numpy as np
from jax import lax
from jax.experimental import pallas as pl
from jax.experimental.pallas import tpu as pltpu
from jax.sharding import PartitionSpec as P

STEPS = 4
MESH = pl.DeviceIdType.MESH

LEVELS, BAND, NLON, NLAT = 20, 8, 768, 256
CHUNKS = 4
PER = LEVELS // CHUNKS
TILE = 128
TILES = NLON // TILE
HALF_TILES = TILES // 2
UNITS = TILES * PER
HALF_UNITS = UNITS // 2
PEERS = NLAT // BAND
SHARE = NLON // PEERS


def lat_of(half, column):
    return ((column // 4) * 2 + half) * 4 + column % 4


def split_bf16(table):
    high = table.astype(jnp.bfloat16)
    low = (table - high.astype(np.float64)).astype(jnp.bfloat16)
    return high, low


def column_order():
    order = []
    for half in range(2):
        for tile in range(HALF_TILES):
            for column in range(5 * tile, 5 * tile + 5):
                order += [lat_of(half, column) * SHARE + i for i in range(SHARE)]
            order += [lat_of(half, 15) * SHARE + 8 * tile + i for i in range(8)]
    return np.array(order)


def tables():
    half_count = NLON // 2
    points = np.arange(NLON)[:, None]
    orders = np.arange(half_count)[None, :]
    angles = (points * orders % NLON) * (2.0 * math.pi / NLON)
    forward = np.concatenate([np.cos(angles), np.sin(angles)], axis=1)
    weights = np.where(orders == 0, 1.0, 2.0) / NLON
    backward = (forward * np.concatenate([weights, weights], axis=1)).T
    order = column_order()
    modes = np.arange(NLAT)[:, None]
    lats = np.arange(NLAT)[None, :]
    angles = ((2 * lats + 1) * modes % (4 * NLAT)) * (math.pi / (2 * NLAT))
    scaling = np.where(modes == 0, math.sqrt(1.0 / NLAT), math.sqrt(2.0 / NLAT))
    basis = scaling * np.cos(angles)
    return (
        *split_bf16(forward[:, order]),
        *split_bf16(backward[order, :]),
        *split_bf16(basis),
        *split_bf16(np.ascontiguousarray(basis.T)),
    )


def dot(a, b):
    return lax.dot_general(a, b, (((1,), (0,)), ((), ())), preferred_element_type=jnp.float32)


def rows_times_table(rows, high, low):
    count = rows.shape[0]
    rows_high = rows.astype(jnp.bfloat16).astype(jnp.float32)
    both = jnp.concatenate([rows_high, rows - rows_high], axis=0).astype(jnp.bfloat16)
    wide = dot(both, high)
    return wide[:count] + wide[count:] + dot(rows_high.astype(jnp.bfloat16), low)


def table_times_columns(high, low, columns):
    count = columns.shape[1]
    columns_high = columns.astype(jnp.bfloat16).astype(jnp.float32)
    both = jnp.concatenate([columns_high, columns - columns_high], axis=1).astype(jnp.bfloat16)
    wide = dot(high, both)
    return wide[:, :count] + wide[:, count:] + dot(low, columns_high.astype(jnp.bfloat16))


def kernel(
    pert, lat_off, lon_off, lat_w, lon_w, var,
    fwd_high, fwd_low, bwd_high, bwd_low, basis_high, basis_low, basis_t_high, basis_t_low,
    out,
    field, from_south, from_north, prev, coeffs, owned, answer, returned, var_rows, var_tile,
    halo_send, halo_recv, shift_send, shift_recv, out_send, out_recv, back_send, back_recv, var_send, var_recv,
):
    win = lax.axis_index("win")
    lat = lax.axis_index("lat")
    windows = lax.axis_size("win")
    half = (lat // 4) % 2
    column = (lat // 8) * 4 + lat % 4
    my_unit = half * HALF_UNITS + column
    owner = column < HALF_UNITS
    has_south = lat > 0
    has_north = lat < PEERS - 1
    has_prior = win > 0
    has_next = win < windows - 1

    barrier = pltpu.get_barrier_semaphore()

    @pl.loop(0, PEERS)
    def _(peer):
        @pl.when(peer != lat)
        def _():
            pl.semaphore_signal(barrier, 1, device_id={"lat": peer}, device_id_type=MESH)

    @pl.when(has_prior)
    def _():
        pl.semaphore_signal(barrier, 1, device_id={"win": win - 1}, device_id_type=MESH)

    @pl.when(has_next)
    def _():
        pl.semaphore_signal(barrier, 1, device_id={"win": win + 1}, device_id_type=MESH)

    @pl.when(jnp.logical_not(has_south))
    def _():
        from_south[...] = jnp.zeros_like(from_south)

    @pl.when(jnp.logical_not(has_north))
    def _():
        from_north[...] = jnp.zeros_like(from_north)

    pl.semaphore_wait(barrier, PEERS - 1 + has_prior.astype(jnp.int32) + has_next.astype(jnp.int32))

    def source(step):
        return pert if step == 0 else field.at[step - 1]

    def to_north(step, chunk):
        levels = pl.ds(chunk * PER, PER)
        return pltpu.make_async_remote_copy(
            source(step).at[levels, pl.ds(BAND - 1, 1)], from_south.at[step, levels, pl.ds(BAND - 1, 1)],
            halo_send.at[0, step, chunk], halo_recv.at[0, step, chunk],
            device_id={"lat": lat + 1}, device_id_type=MESH)

    def to_south(step, chunk):
        levels = pl.ds(chunk * PER, PER)
        return pltpu.make_async_remote_copy(
            source(step).at[levels, pl.ds(0, 1)], from_north.at[step, levels, pl.ds(0, 1)],
            halo_send.at[1, step, chunk], halo_recv.at[1, step, chunk],
            device_id={"lat": lat - 1}, device_id_type=MESH)

    def send_halo(step, chunk):
        @pl.when(has_north)
        def _():
            to_north(step, chunk).start()

        @pl.when(has_south)
        def _():
            to_south(step, chunk).start()

    for chunk in range(CHUNKS):
        send_halo(0, chunk)

    def share_copy(tile, level):
        target = lat_of(half, tile * 5 + level)
        return target, var, var_rows.at[pl.ds(pl.multiple_of((column % 5) * SHARE, 8), SHARE)], var_recv.at[column % 5]

    @pl.when(owner)
    def _():
        for level in range(PER):
            tile = column // 5
            target = lat_of(half, tile * 5 + level)
            landing = var_rows.at[pl.ds(pl.multiple_of((column % 5) * SHARE, 8), SHARE)]

            @pl.when(target != lat)
            def _():
                pltpu.make_async_remote_copy(
                    var, landing, var_send, var_recv.at[column % 5],
                    device_id={"lat": target}, device_id_type=MESH).start()

            @pl.when(target == lat)
            def _():
                pltpu.make_async_copy(var, landing, var_recv.at[column % 5]).start()

    @pl.when(jnp.logical_not(owner))
    def _():
        for tile in range(HALF_TILES):
            for level in range(PER):
                pltpu.make_async_remote_copy(
                    var.at[pl.ds(8 * tile, 8)], var_rows.at[pl.ds(5 * SHARE, 8)], var_send, var_recv.at[5],
                    device_id={"lat": lat_of(half, tile * 5 + level)}, device_id_type=MESH).start()

    rows_at = lax.broadcasted_iota(jnp.int32, (BAND, NLON), 0)
    lane = lax.broadcasted_iota(jnp.int32, (BAND, TILE), 1)

    def advance(step, level):
        here = source(step)[level]
        south = pltpu.roll(
            jnp.where(rows_at == BAND - 1, from_south[step, level, pl.ds(BAND - 1, 1)], here), 1, 0)
        north = pltpu.roll(
            jnp.where(rows_at == 0, from_north[step, level, pl.ds(0, 1)], here), BAND - 1, 0)
        for tile in range(TILES):
            cut = slice(tile * TILE, (tile + 1) * TILE)
            west = lane + lon_off[level, :, cut]
            east = west + 1
            west_in = (west >= 0) & (west < TILE)
            east_in = (east >= 0) & (east < TILE)
            west = west & (TILE - 1)
            east = east & (TILE - 1)
            weight = lon_w[level, :, cut]
            mixed = []
            for rows in (south, here, north):
                middle = rows[:, cut]
                after = (tile + 1) % TILES * TILE
                before = (tile - 1) % TILES * TILE
                beside = jnp.where(
                    lane < TILE // 2, rows[:, after : after + TILE], rows[:, before : before + TILE])
                near = jnp.where(
                    west_in, jnp.take_along_axis(middle, west, 1), jnp.take_along_axis(beside, west, 1))
                far = jnp.where(
                    east_in, jnp.take_along_axis(middle, east, 1), jnp.take_along_axis(beside, east, 1))
                mixed.append((1.0 - weight) * near + weight * far)
            below = lat_off[level, :, cut] < 0
            lower = jnp.where(below, mixed[0], mixed[1])
            upper = jnp.where(below, mixed[1], mixed[2])
            part = lat_w[level, :, cut]
            field[step, level, :, cut] = (1.0 - part) * lower + part * upper

    def shift(chunk):
        levels = pl.ds(chunk * PER, PER)
        return pltpu.make_async_remote_copy(
            field.at[STEPS - 1, levels], prev.at[levels], shift_send.at[chunk], shift_recv.at[chunk],
            device_id={"win": win + 1}, device_id_type=MESH)

    for step in range(STEPS):
        for chunk in range(CHUNKS):
            @pl.when(has_south)
            def _():
                to_north(step, chunk).wait_recv()

            @pl.when(has_north)
            def _():
                to_south(step, chunk).wait_recv()

            @pl.loop(chunk * PER, (chunk + 1) * PER)
            def _(level):
                advance(step, level)

            if step < STEPS - 1:
                send_halo(step + 1, chunk)
            else:
                @pl.when(has_next)
                def _():
                    shift(chunk).start()

    my_rows = pl.ds(pl.multiple_of(lat * BAND, BAND), BAND)

    for chunk in range(CHUNKS):
        levels = pl.ds(chunk * PER, PER)

        @pl.when(has_prior)
        def _():
            shift(chunk).wait_recv()

        @pl.when(jnp.logical_not(has_prior))
        def _():
            prev[levels] = jnp.zeros((PER, BAND, NLON), jnp.float32)

        error = (pert[levels] - prev[levels]).reshape(PER * BAND, NLON)
        result = rows_times_table(error, fwd_high[...], fwd_low[...])
        for tile in range(TILES):
            coeffs[chunk, pl.ds(tile * PER, PER)] = result[:, tile * TILE : (tile + 1) * TILE].reshape(
                PER, BAND, TILE)

        @pl.loop(0, UNITS)
        def _(unit):
            target = lat_of(unit // HALF_UNITS, unit % HALF_UNITS)

            @pl.when(target != lat)
            def _():
                pltpu.make_async_remote_copy(
                    coeffs.at[chunk, unit], owned.at[chunk, my_rows], out_send.at[chunk], out_recv.at[chunk],
                    device_id={"lat": target}, device_id_type=MESH).start()

            @pl.when(target == lat)
            def _():
                pltpu.make_async_copy(
                    coeffs.at[chunk, unit], owned.at[chunk, my_rows], out_recv.at[chunk]).start()

    @pl.when(owner)
    def _():
        for share in range(5):
            piece = var_rows.at[pl.ds(share * SHARE, SHARE)]
            pltpu.make_async_copy(piece, piece, var_recv.at[share]).wait()
        piece = var_rows.at[pl.ds(5 * SHARE, 8)]
        pltpu.make_async_copy(piece, piece, var_recv.at[5]).wait()
        var_tile[...] = var_rows[...].T

        for chunk in range(CHUNKS):
            pltpu.make_async_copy(owned.at[chunk], owned.at[chunk], out_recv.at[chunk]).wait()
            modes = table_times_columns(basis_high[...], basis_low[...], owned[chunk])
            answer[chunk] = table_times_columns(
                basis_t_high[...], basis_t_low[...], modes * var_tile[...])

            @pl.loop(0, PEERS)
            def _(peer):
                rows = pl.ds(pl.multiple_of(peer * BAND, BAND), BAND)

                @pl.when(peer != lat)
                def _():
                    pltpu.make_async_remote_copy(
                        answer.at[chunk, rows], returned.at[chunk, my_unit], back_send.at[chunk],
                        back_recv.at[chunk], device_id={"lat": peer}, device_id_type=MESH).start()

                @pl.when(peer == lat)
                def _():
                    pltpu.make_async_copy(
                        answer.at[chunk, rows], returned.at[chunk, my_unit], back_recv.at[chunk]).start()

    for chunk in range(CHUNKS):
        pltpu.make_async_copy(returned.at[chunk], returned.at[chunk], back_recv.at[chunk]).wait()
        rows = jnp.concatenate(
            [returned[chunk, pl.ds(tile * PER, PER)].reshape(PER * BAND, TILE) for tile in range(TILES)], axis=1)
        result = rows_times_table(rows, bwd_high[...], bwd_low[...])
        out[pl.ds(chunk * PER, PER)] = result.reshape(PER, BAND, NLON)

    for step in range(STEPS):
        for chunk in range(CHUNKS):
            @pl.when(has_north)
            def _():
                to_north(step, chunk).wait_send()

            @pl.when(has_south)
            def _():
                to_south(step, chunk).wait_send()

    for chunk in range(CHUNKS):
        @pl.when(has_next)
        def _():
            shift(chunk).wait_send()

        @pl.when(owner)
        def _():
            part = coeffs.at[chunk, pl.ds(0, UNITS - 1)]
            pltpu.make_async_copy(part, part, out_send.at[chunk]).wait()
            part = answer.at[chunk, pl.ds(0, NLAT - BAND)]
            pltpu.make_async_copy(part, part, back_send.at[chunk]).wait()

        @pl.when(jnp.logical_not(owner))
        def _():
            part = coeffs.at[chunk]
            pltpu.make_async_copy(part, part, out_send.at[chunk]).wait()

    @pl.when(owner)
    def _():
        part = var_rows.at[pl.ds(0, 4 * SHARE)]
        pltpu.make_async_copy(part, part, var_send).wait()

    @pl.when(jnp.logical_not(owner))
    def _():
        part = var_rows.at[pl.ds(0, HALF_TILES * PER * 8)]
        pltpu.make_async_copy(part, part, var_send).wait()


def body(perturbation, lat_offset, lon_offset, lat_weight, lon_weight, spectral_var):
    def levels_first(x):
        return jnp.transpose(x[0], (1, 0, 2))

    grid = (LEVELS, BAND, NLON)
    f32 = jnp.float32
    dma = pltpu.SemaphoreType.DMA
    vmem = pl.BlockSpec(memory_space=pltpu.VMEM)
    constants = [jnp.asarray(table) for table in tables()]
    result = pl.pallas_call(
        kernel,
        out_shape=jax.ShapeDtypeStruct(grid, f32),
        in_specs=[vmem] * (6 + len(constants)),
        out_specs=vmem,
        scratch_shapes=[
            pltpu.VMEM((STEPS, *grid), f32),
            pltpu.VMEM((STEPS, *grid), f32),
            pltpu.VMEM((STEPS, *grid), f32),
            pltpu.VMEM(grid, f32),
            pltpu.VMEM((CHUNKS, UNITS, BAND, TILE), f32),
            pltpu.VMEM((CHUNKS, NLAT, TILE), f32),
            pltpu.VMEM((CHUNKS, NLAT, TILE), f32),
            pltpu.VMEM((CHUNKS, UNITS, BAND, TILE), f32),
            pltpu.VMEM((TILE, NLAT), f32),
            pltpu.VMEM((NLAT, TILE), f32),
            dma((2, STEPS, CHUNKS)),
            dma((2, STEPS, CHUNKS)),
            dma((CHUNKS,)),
            dma((CHUNKS,)),
            dma((CHUNKS,)),
            dma((CHUNKS,)),
            dma((CHUNKS,)),
            dma((CHUNKS,)),
            dma,
            dma((6,)),
        ],
        compiler_params=pltpu.CompilerParams(
            collective_id=0, has_side_effects=True, vmem_limit_bytes=48 * 2**20),
    )(
        *[levels_first(x) for x in (perturbation, lat_offset, lon_offset, lat_weight, lon_weight)],
        spectral_var.T,
        *constants,
    )
    return jnp.transpose(result, (1, 0, 2))[None]


def solution(mesh):
    block = P("win", "lat", None, None)
    return jax.shard_map(
        body, mesh=mesh, in_specs=(block, block, block, block, block, P(None, "lat")), out_specs=block,
        check_vma=False)
```

profile of v0, /device:TPU:449, one launch (start us, length us, event | category | flops | bytes accessed | tf_op | source)
XLA Modules:
  0.0 127.1 jit_solution(17275818984957514181)
XLA Ops:
  0.0 0.0 copy-start
  0.0 1.3 copy-done
  1.3 0.0 copy-start.1
  1.3 1.3 copy-done.1
  2.5 0.0 copy-start.2
  2.5 1.0 copy-done.2
  3.6 0.0 copy-start.3
  3.6 1.0 copy-done.3
  4.6 0.0 copy-start.4
  4.6 1.0 copy-done.4
  5.6 0.0 copy-start.5
  5.6 1.0 copy-done.5
  6.7 0.0 copy-start.6
  6.7 1.0 copy-done.6
  7.7 0.0 copy-start.7
  7.7 0.9 copy-done.7
  8.6 0.0 copy-start.8
  8.6 0.9 copy-done.8
  9.5 0.0 copy-start.9
  9.5 0.9 copy-done.9
  10.4 0.0 copy-start.10
  10.4 0.9 copy-done.10
  11.3 0.0 copy-start.11
  11.3 0.7 copy-done.11
  12.1 114.2 %shard_map.136 = f32[20,8,768]{2,1,0:T(8,128)S(1)} custom-call(f32[20,8,768]{2,1,0:T(8,128)S(1)} %bitcast.20, s32[20,8,768]{2,1,0:T(8,128)S(1)} %bitcast.21, s32[20,8,768]{2,1,0:T(8,128)S(1)} %bitcast.22, f32[20,8,768]{2,1,0:T(8,128)S(1)} %bitcast.23, f32[20,8,768]{2,1,0:T(8,128)S(1)} %bitcast.24, f32[24,256]{1,0:T(8,128)S(1)} %bitcast.25, ...), custom_call_target="tpu_custom_call" | custom-call | tf_op jit(solution)/shard_map/pallas_call | solution.py:372
  126.3 0.8 copy.16
Async XLA Ops:
  0.0 1.3 copy-start
  1.3 1.3 copy-start.1
  2.5 1.0 copy-start.2
  3.6 1.0 copy-start.3
  4.6 1.0 copy-start.4
  5.6 1.0 copy-start.5
  6.7 1.0 copy-start.6
  7.7 0.9 copy-start.7
  8.6 0.9 copy-start.8
  9.5 0.9 copy-start.9
  10.4 0.9 copy-start.10
  11.3 0.7 copy-start.11
where the time goes:
time: 128 us; the launch traced here: 127 us
  Pallas kernels  114 us (89%)
  local copies, waits for them, and re-layouts  12.8 us (10%)
    pallas_call x1, Pallas kernels, body(): pl.pallas_call(kernel, out_shape=jax.ShapeDtypeStruct(grid, f32), in_spec...  114 us
    unnamed x25, local copies, waits for them, and re-layouts  12.8 us

commit v1 on v0

--- a/solution.py
+++ b/solution.py
@@ -21,6 +21,7 @@
 HALF_UNITS = UNITS // 2
 PEERS = NLAT // BAND
 SHARE = NLON // PEERS
+FETCHED = 14
 
 
 def lat_of(half, column):
@@ -86,12 +87,23 @@
 
 
 def kernel(
-    pert, lat_off, lon_off, lat_w, lon_w, var,
-    fwd_high, fwd_low, bwd_high, bwd_low, basis_high, basis_low, basis_t_high, basis_t_low,
-    out,
-    field, from_south, from_north, prev, coeffs, owned, answer, returned, var_rows, var_tile,
-    halo_send, halo_recv, shift_send, shift_recv, out_send, out_recv, back_send, back_recv, var_send, var_recv,
+    *refs,
 ):
+    sources, (out, *fetched), rest = refs[:FETCHED], refs[FETCHED : 2 * FETCHED + 1], refs[2 * FETCHED + 1 :]
+    (pert, lat_off, lon_off, lat_w, lon_w, var,
+     fwd_high, fwd_low, bwd_high, bwd_low, basis_high, basis_low, basis_t_high, basis_t_low) = fetched
+    (
+        field, from_south, from_north, prev, coeffs, owned, answer, returned, var_rows, var_tile,
+        halo_send, halo_recv, shift_send, shift_recv, out_send, out_recv, back_send, back_recv, var_send, var_recv,
+        fetch_sem,
+    ) = rest
+    fetches = [
+        pltpu.make_async_copy(source, target, fetch_sem.at[i])
+        for i, (source, target) in enumerate(zip(sources, fetched))
+    ]
+    for fetch in fetches:
+        fetch.start()
+
     win = lax.axis_index("win")
     lat = lax.axis_index("lat")
     windows = lax.axis_size("win")
@@ -99,10 +111,10 @@
     column = (lat // 8) * 4 + lat % 4
     my_unit = half * HALF_UNITS + column
     owner = column < HALF_UNITS
-    has_south = lat > 0
-    has_north = lat < PEERS - 1
     has_prior = win > 0
     has_next = win < windows - 1
+    has_south = has_next & (lat > 0)
+    has_north = has_next & (lat < PEERS - 1)
 
     barrier = pltpu.get_barrier_semaphore()
 
@@ -128,6 +140,8 @@
     def _():
         from_north[...] = jnp.zeros_like(from_north)
 
+    for fetch in fetches[:6]:
+        fetch.wait()
     pl.semaphore_wait(barrier, PEERS - 1 + has_prior.astype(jnp.int32) + has_next.astype(jnp.int32))
 
     def source(step):
@@ -158,10 +172,6 @@
 
     for chunk in range(CHUNKS):
         send_halo(0, chunk)
-
-    def share_copy(tile, level):
-        target = lat_of(half, tile * 5 + level)
-        return target, var, var_rows.at[pl.ds(pl.multiple_of((column % 5) * SHARE, 8), SHARE)], var_recv.at[column % 5]
 
     @pl.when(owner)
     def _():
@@ -240,9 +250,11 @@
             def _():
                 to_south(step, chunk).wait_recv()
 
-            @pl.loop(chunk * PER, (chunk + 1) * PER)
-            def _(level):
-                advance(step, level)
+            @pl.when(has_next)
+            def _():
+                @pl.loop(chunk * PER, (chunk + 1) * PER)
+                def _(level):
+                    advance(step, level)
 
             if step < STEPS - 1:
                 send_halo(step + 1, chunk)
@@ -251,6 +263,9 @@
                 def _():
                     shift(chunk).start()
 
+    for fetch in fetches[6:]:
+        fetch.wait()
+
     my_rows = pl.ds(pl.multiple_of(lat * BAND, BAND), BAND)
 
     for chunk in range(CHUNKS):
@@ -367,14 +382,18 @@
     grid = (LEVELS, BAND, NLON)
     f32 = jnp.float32
     dma = pltpu.SemaphoreType.DMA
-    vmem = pl.BlockSpec(memory_space=pltpu.VMEM)
-    constants = [jnp.asarray(table) for table in tables()]
+    operands = [
+        *[levels_first(x) for x in (perturbation, lat_offset, lon_offset, lat_weight, lon_weight)],
+        spectral_var.T,
+        *[jnp.asarray(table) for table in tables()],
+    ]
     result = pl.pallas_call(
         kernel,
         out_shape=jax.ShapeDtypeStruct(grid, f32),
-        in_specs=[vmem] * (6 + len(constants)),
-        out_specs=vmem,
+        in_specs=[pl.BlockSpec(memory_space=pl.ANY)] * FETCHED,
+        out_specs=pl.BlockSpec(memory_space=pltpu.VMEM),
         scratch_shapes=[
+            *[pltpu.VMEM(x.shape, x.dtype) for x in operands],
             pltpu.VMEM((STEPS, *grid), f32),
             pltpu.VMEM((STEPS, *grid), f32),
             pltpu.VMEM((STEPS, *grid), f32),
@@ -395,14 +414,11 @@
             dma((CHUNKS,)),
             dma,
             dma((6,)),
+            dma((FETCHED,)),
         ],
         compiler_params=pltpu.CompilerParams(
-            collective_id=0, has_side_effects=True, vmem_limit_bytes=48 * 2**20),
-    )(
-        *[levels_first(x) for x in (perturbation, lat_offset, lon_offset, lat_weight, lon_weight)],
-        spectral_var.T,
-        *constants,
-    )
+            collective_id=0, has_side_effects=True, vmem_limit_bytes=60 * 2**20),
+    )(*operands)
     return jnp.transpose(result, (1, 0, 2))[None]
 
 

time: 128 us -> 116 us (0.906)
  local copies, waits for them, and re-layouts: 12.8 us -> 1.84 us
    unnamed x25 -> x1, local copies, waits for them, and re-layouts: 12.8 us -> 1.84 us
where the time goes in v1:
time: 116 us
  Pallas kernels  114 us (98%)
  local copies, waits for them, and re-layouts  1.84 us (2%)
    pallas_call x1, Pallas kernels, body(): pl.pallas_call(kernel, out_shape=jax.ShapeDtypeStruct(grid, f32), in_spec...  114 us

profile of v1, /device:TPU:449, one launch (start us, length us, event | category | flops | bytes accessed | tf_op | source)
XLA Modules:
  0.0 115.6 jit_solution(11775927005675896238)
XLA Ops:
  0.0 113.7 %shard_map.136 = f32[20,8,768]{2,1,0:T(8,128)} custom-call(f32[20,8,768]{2,1,0:T(8,128)} %bitcast.20, s32[20,8,768]{2,1,0:T(8,128)} %bitcast.21, s32[20,8,768]{2,1,0:T(8,128)} %bitcast.22, f32[20,8,768]{2,1,0:T(8,128)} %bitcast.23, f32[20,8,768]{2,1,0:T(8,128)} %bitcast.24, f32[24,256]{1,0:T(8,128)} %bitcast.25, bf16[768,768]{1,0:T(8,128)(2,1)} %constant.16.clone.refs_6_, ...), custom_call_target="tpu_custom_call" | custom-call | tf_op jit(solution)/shard_map/pallas_call | solution.py:390
  113.7 1.8 %copy.16 = f32[1,8,20,768]{3,1,2,0:T(8,128)} copy(f32[1,8,20,768]{3,1,2,0:T(8,128)} %bitcast.19) | data formatting | bytes 983040

commit v2 on v1

--- a/solution.py
+++ b/solution.py
@@ -12,7 +12,7 @@
 MESH = pl.DeviceIdType.MESH
 
 LEVELS, BAND, NLON, NLAT = 20, 8, 768, 256
-CHUNKS = 4
+CHUNKS = 5
 PER = LEVELS // CHUNKS
 TILE = 128
 TILES = NLON // TILE
@@ -25,7 +25,14 @@
 
 
 def lat_of(half, column):
-    return ((column // 4) * 2 + half) * 4 + column % 4
+    inner = column < 8
+    x = inner * (column // 2) + (1 - inner) * (column % 4)
+    y = inner * (1 + column % 2) + (1 - inner) * (column // 12) * 3
+    return (x * 2 + half) * 4 + y
+
+
+def owner_of(half, place, chunk):
+    return lat_of(half, place + 4 * (chunk % 2) * (place // 8))
 
 
 def split_bf16(table):
@@ -108,9 +115,14 @@
     lat = lax.axis_index("lat")
     windows = lax.axis_size("win")
     half = (lat // 4) % 2
-    column = (lat // 8) * 4 + lat % 4
-    my_unit = half * HALF_UNITS + column
-    owner = column < HALF_UNITS
+    x, y = lat // 8, lat % 4
+    column = jnp.where(y == 0, 8 + x, jnp.where(y == 3, 12 + x, 2 * x + y - 1))
+    inner = column < 8
+    my_unit = half * HALF_UNITS + jnp.where(inner, column, 8 + x)
+
+    def owns(chunk):
+        return inner | (y == 0 if chunk % 2 == 0 else y == 3)
+
     has_prior = win > 0
     has_next = win < windows - 1
     has_south = has_next & (lat > 0)
@@ -173,30 +185,44 @@
     for chunk in range(CHUNKS):
         send_halo(0, chunk)
 
-    @pl.when(owner)
-    def _():
-        for level in range(PER):
-            tile = column // 5
-            target = lat_of(half, tile * 5 + level)
-            landing = var_rows.at[pl.ds(pl.multiple_of((column % 5) * SHARE, 8), SHARE)]
+    whole = column < 15
+    share_tile = column // 5
+    share_first = share_tile * PER
+    share_count = jnp.where(share_tile == 2, 2 * PER, PER)
+    landing = var_rows.at[pl.ds(pl.multiple_of((column % 5) * SHARE, 8), SHARE)]
+    rest_landing = var_rows.at[pl.ds(5 * SHARE, 8)]
+
+    def share_to(target, i):
+        return pltpu.make_async_remote_copy(
+            var, landing, var_send.at[i], var_recv.at[column % 5], device_id={"lat": target}, device_id_type=MESH)
+
+    def rest_to(target, i):
+        tile = jnp.minimum(i // PER, 2)
+        return pltpu.make_async_remote_copy(
+            var.at[pl.ds(pl.multiple_of(8 * tile, 8), 8)], rest_landing, var_send.at[i], var_recv.at[5],
+            device_id={"lat": target}, device_id_type=MESH)
+
+    @pl.when(whole)
+    def _():
+        @pl.loop(0, share_count)
+        def _(i):
+            target = lat_of(half, share_first + i)
 
             @pl.when(target != lat)
             def _():
-                pltpu.make_async_remote_copy(
-                    var, landing, var_send, var_recv.at[column % 5],
-                    device_id={"lat": target}, device_id_type=MESH).start()
+                share_to(target, i).start()
 
             @pl.when(target == lat)
             def _():
                 pltpu.make_async_copy(var, landing, var_recv.at[column % 5]).start()
 
-    @pl.when(jnp.logical_not(owner))
-    def _():
-        for tile in range(HALF_TILES):
-            for level in range(PER):
-                pltpu.make_async_remote_copy(
-                    var.at[pl.ds(8 * tile, 8)], var_rows.at[pl.ds(5 * SHARE, 8)], var_send, var_recv.at[5],
-                    device_id={"lat": lat_of(half, tile * 5 + level)}, device_id_type=MESH).start()
+    @pl.when(jnp.logical_not(whole))
+    def _():
+        @pl.loop(0, 15)
+        def _(i):
+            rest_to(lat_of(half, i), i).start()
+
+        pltpu.make_async_copy(var.at[pl.ds(16, 8)], rest_landing, var_recv.at[5]).start()
 
     rows_at = lax.broadcasted_iota(jnp.int32, (BAND, NLON), 0)
     lane = lax.broadcasted_iota(jnp.int32, (BAND, TILE), 1)
@@ -286,8 +312,11 @@
                 PER, BAND, TILE)
 
         @pl.loop(0, UNITS)
-        def _(unit):
-            target = lat_of(unit // HALF_UNITS, unit % HALF_UNITS)
+        def _(turn):
+            side = jnp.where(turn < HALF_UNITS, 1 - half, half)
+            place = (turn + column) % HALF_UNITS
+            unit = side * HALF_UNITS + place
+            target = owner_of(side, place, chunk)
 
             @pl.when(target != lat)
             def _():
@@ -300,23 +329,23 @@
                 pltpu.make_async_copy(
                     coeffs.at[chunk, unit], owned.at[chunk, my_rows], out_recv.at[chunk]).start()
 
-    @pl.when(owner)
-    def _():
-        for share in range(5):
-            piece = var_rows.at[pl.ds(share * SHARE, SHARE)]
-            pltpu.make_async_copy(piece, piece, var_recv.at[share]).wait()
-        piece = var_rows.at[pl.ds(5 * SHARE, 8)]
-        pltpu.make_async_copy(piece, piece, var_recv.at[5]).wait()
-        var_tile[...] = var_rows[...].T
-
-        for chunk in range(CHUNKS):
+    for share in range(5):
+        piece = var_rows.at[pl.ds(share * SHARE, SHARE)]
+        pltpu.make_async_copy(piece, piece, var_recv.at[share]).wait()
+    pltpu.make_async_copy(rest_landing, rest_landing, var_recv.at[5]).wait()
+    var_tile[...] = var_rows[...].T
+
+    for chunk in range(CHUNKS):
+        @pl.when(owns(chunk))
+        def _():
             pltpu.make_async_copy(owned.at[chunk], owned.at[chunk], out_recv.at[chunk]).wait()
             modes = table_times_columns(basis_high[...], basis_low[...], owned[chunk])
             answer[chunk] = table_times_columns(
                 basis_t_high[...], basis_t_low[...], modes * var_tile[...])
 
             @pl.loop(0, PEERS)
-            def _(peer):
+            def _(turn):
+                peer = lat_of(jnp.where(turn < PEERS // 2, 1 - half, half), (turn + column) % (PEERS // 2))
                 rows = pl.ds(pl.multiple_of(peer * BAND, BAND), BAND)
 
                 @pl.when(peer != lat)
@@ -352,27 +381,33 @@
         def _():
             shift(chunk).wait_send()
 
-        @pl.when(owner)
+        @pl.when(owns(chunk))
         def _():
             part = coeffs.at[chunk, pl.ds(0, UNITS - 1)]
             pltpu.make_async_copy(part, part, out_send.at[chunk]).wait()
             part = answer.at[chunk, pl.ds(0, NLAT - BAND)]
             pltpu.make_async_copy(part, part, back_send.at[chunk]).wait()
 
-        @pl.when(jnp.logical_not(owner))
+        @pl.when(jnp.logical_not(owns(chunk)))
         def _():
             part = coeffs.at[chunk]
             pltpu.make_async_copy(part, part, out_send.at[chunk]).wait()
 
-    @pl.when(owner)
-    def _():
-        part = var_rows.at[pl.ds(0, 4 * SHARE)]
-        pltpu.make_async_copy(part, part, var_send).wait()
-
-    @pl.when(jnp.logical_not(owner))
-    def _():
-        part = var_rows.at[pl.ds(0, HALF_TILES * PER * 8)]
-        pltpu.make_async_copy(part, part, var_send).wait()
+    @pl.when(whole)
+    def _():
+        @pl.loop(0, share_count)
+        def _(i):
+            target = lat_of(half, share_first + i)
+
+            @pl.when(target != lat)
+            def _():
+                share_to(target, i).wait_send()
+
+    @pl.when(jnp.logical_not(whole))
+    def _():
+        @pl.loop(0, 15)
+        def _(i):
+            rest_to(lat_of(half, i), i).wait_send()
 
 
 def body(perturbation, lat_offset, lon_offset, lat_weight, lon_weight, spectral_var):
@@ -412,7 +447,7 @@
             dma((CHUNKS,)),
             dma((CHUNKS,)),
             dma((CHUNKS,)),
-            dma,
+            dma((15,)),
             dma((6,)),
             dma((FETCHED,)),
         ],

time: 116 us -> 116 us (level)
  the two profiles are of different devices: /device:TPU:449 before, /device:TPU:40 now
where the time goes in v2:
time: 116 us
  Pallas kernels  114 us (98%)
  local copies, waits for them, and re-layouts  1.84 us (2%)
    pallas_call x1, Pallas kernels, body(): pl.pallas_call(kernel, out_shape=jax.ShapeDtypeStruct(grid, f32), in_spec...  114 us

profile of v2, /device:TPU:40, one launch (start us, length us, event | category | flops | bytes accessed | tf_op | source)
XLA Modules:
  0.0 115.8 jit_solution(8875775531297460180)
XLA Ops:
  0.0 114.0 %shard_map.136 = f32[20,8,768]{2,1,0:T(8,128)} custom-call(f32[20,8,768]{2,1,0:T(8,128)} %bitcast.20, s32[20,8,768]{2,1,0:T(8,128)} %bitcast.21, s32[20,8,768]{2,1,0:T(8,128)} %bitcast.22, f32[20,8,768]{2,1,0:T(8,128)} %bitcast.23, f32[20,8,768]{2,1,0:T(8,128)} %bitcast.24, f32[24,256]{1,0:T(8,128)} %bitcast.25, bf16[768,768]{1,0:T(8,128)(2,1)} %constant.16.clone.refs_6_, ...), custom_call_target="tpu_custom_call" | custom-call | tf_op jit(solution)/shard_map/pallas_call | solution.py:425
  114.0 1.8 %copy.16 = f32[1,8,20,768]{3,1,2,0:T(8,128)} copy(f32[1,8,20,768]{3,1,2,0:T(8,128)} %bitcast.19) | data formatting | bytes 983040

commit v3 on v2

--- a/solution.py
+++ b/solution.py
@@ -108,8 +108,7 @@
         pltpu.make_async_copy(source, target, fetch_sem.at[i])
         for i, (source, target) in enumerate(zip(sources, fetched))
     ]
-    for fetch in fetches:
-        fetch.start()
+    fetches[0].start()
 
     win = lax.axis_index("win")
     lat = lax.axis_index("lat")
@@ -131,7 +130,9 @@
     barrier = pltpu.get_barrier_semaphore()
 
     @pl.loop(0, PEERS)
-    def _(peer):
+    def _(turn):
+        peer = lat_of(jnp.where(turn < PEERS // 2, 1 - half, half), turn % (PEERS // 2))
+
         @pl.when(peer != lat)
         def _():
             pl.semaphore_signal(barrier, 1, device_id={"lat": peer}, device_id_type=MESH)
@@ -144,6 +145,9 @@
     def _():
         pl.semaphore_signal(barrier, 1, device_id={"win": win + 1}, device_id_type=MESH)
 
+    for fetch in fetches[1:]:
+        fetch.start()
+
     @pl.when(jnp.logical_not(has_south))
     def _():
         from_south[...] = jnp.zeros_like(from_south)
@@ -152,8 +156,7 @@
     def _():
         from_north[...] = jnp.zeros_like(from_north)
 
-    for fetch in fetches[:6]:
-        fetch.wait()
+    fetches[0].wait()
     pl.semaphore_wait(barrier, PEERS - 1 + has_prior.astype(jnp.int32) + has_next.astype(jnp.int32))
 
     def source(step):
@@ -184,6 +187,9 @@
 
     for chunk in range(CHUNKS):
         send_halo(0, chunk)
+
+    for fetch in fetches[1:6]:
+        fetch.wait()
 
     whole = column < 15
     share_tile = column // 5

time: 116 us -> 118 us (1.017)
  the two profiles are of different devices: /device:TPU:40 before, /device:TPU:2 now
where the time goes in v3:
time: 118 us
  Pallas kernels  116 us (98%)
  local copies, waits for them, and re-layouts  1.84 us (2%)
    pallas_call x1, Pallas kernels, body(): pl.pallas_call(kernel, out_shape=jax.ShapeDtypeStruct(grid, f32), in_spec...  116 us

profile of v3, /device:TPU:2, one launch (start us, length us, event | category | flops | bytes accessed | tf_op | source)
XLA Modules:
  0.0 118.2 jit_solution(6732885987347503592)
XLA Ops:
  0.0 116.4 %shard_map.136 = f32[20,8,768]{2,1,0:T(8,128)} custom-call(f32[20,8,768]{2,1,0:T(8,128)} %bitcast.20, s32[20,8,768]{2,1,0:T(8,128)} %bitcast.21, s32[20,8,768]{2,1,0:T(8,128)} %bitcast.22, f32[20,8,768]{2,1,0:T(8,128)} %bitcast.23, f32[20,8,768]{2,1,0:T(8,128)} %bitcast.24, f32[24,256]{1,0:T(8,128)} %bitcast.25, bf16[768,768]{1,0:T(8,128)(2,1)} %constant.16.clone.refs_6_, ...), custom_call_target="tpu_custom_call" | custom-call | tf_op jit(solution)/shard_map/pallas_call | solution.py:431
  116.4 1.8 %copy.16 = f32[1,8,20,768]{3,1,2,0:T(8,128)} copy(f32[1,8,20,768]{3,1,2,0:T(8,128)} %bitcast.19) | data formatting | bytes 983040
